TPU v7x, 32 devices: a whole 2x2x4 slice. The times are simulated.
32 devices in a mesh: groups: 2 (over y), ctx: 4 (over z), dp: 2 (over x), mp: 2 (over core).
Axes of the slice: x: 2, y: 2, z: 4, core: 2. Of those that a mesh axis runs over, the one named last changes fastest.
Arguments:
- head_inputs: bfloat16 [3, 4, 1024, 1536], P(None, ('groups', 'dp'), 'ctx', 'mp'), parts along dimension 1, may hold values from -0.29882812 to 0.29882812
- write_read: bfloat16 [3, 4, 1024, 128], P(None, ('groups', 'dp'), 'ctx'), parts along dimension 1, may hold values from -0.26953125 to 0.26953125
- decay_steps: int32 [3, 4, 12, 1024], P(None, ('groups', 'dp'), 'mp', 'ctx'), parts along dimension 1, may hold values from 0 to 512
- scan_orders: int32 [2, 4, 1024], P(None, ('groups', 'dp'), 'ctx'), parts along dimension 1, may hold values from 0 to 1023, as said below
- cotangent: bfloat16 [4, 1024, 768], P(('groups', 'dp'), 'ctx'), parts along dimension 0, may hold values from -0.59765625 to 0.59765625
- out_weight: bfloat16 [3, 768, 1536], P(None, 'ctx', 'mp'), may hold values from -0.4375 to 0.4375
Outputs:
- grad_inputs: bfloat16 [3, 4, 1024, 1536], P(None, ('groups', 'dp'), 'ctx', 'mp'), parts along dimension 1
- grad_write_read: bfloat16 [3, 4, 1024, 128], P(None, ('groups', 'dp'), 'ctx'), parts along dimension 1
- grad_weight: bfloat16 [6, 768, 1536], P('groups', 'ctx', 'mp'), parts along dimension 0
There are 2 independent parts, one for each index of `groups`. A program takes and returns all parts, laid end to end along the dimension named above; an argument that names none is the same for every part. Nothing has to cross between parts.
Inputs may be any that keep to these rules, and one draw needn't show every extreme that they name: `scan_orders`: for every volume and each of the two orders, position d * 256 + q * 64 + m (0 <= m < 64) holds a patch of index q * 256 + d * 64 + m' with 0 <= m' < 64; every patch stands at exactly one position.
All inputs are finite; a program needn't handle non-finite values.
Results may differ from a plain program's by a relative error of at most 0.005.
Values may be sent and summed in bfloat16 or wider, within the bound.
A program may use at most 128 MiB of HBM per device.

v0:
```python
import math
import jax
import jax.numpy as jnp
from jax import lax
from jax.sharding import PartitionSpec as P

P_SIZE = 128
N = 64
EXACT = lax.Precision.HIGHEST


def prefix(value, axis, join, neutral, backward):
    count, mine = (lax.axis_size(axis), lax.axis_index(axis))
    pieces = jax.tree.map(lambda part: lax.all_gather(part, axis), value)
    if backward:
        pieces = jax.tree.map(lambda part: part[::-1], pieces)
        mine = count - 1 - mine
    running = jax.tree.map(
        lambda part, zero: jnp.full_like(part, 0) + jnp.asarray(zero, part.dtype), value, neutral
    )

    def lap(position, running):
        longer = join(running, jax.tree.map(lambda part: part[position], pieces))
        return jax.tree.map(lambda new, old: jnp.where(position < mine, new, old), longer, running)

    return lax.fori_loop(0, count - 1, lap, running)


def contract(form, *operands):
    return jnp.einsum(form, *operands, precision=EXACT)


def segment_parts(log_rates, writes, readers):
    running = jnp.cumsum(log_rates, axis=-1)
    final_log = running[..., -1]
    length = log_rates.shape[-1]
    causal = jnp.arange(length)[:, None] >= jnp.arange(length)[None, :]
    differ = jnp.where(causal, running[..., :, None] - running[..., None, :], 0.0)
    decay_mat = jnp.where(causal, jnp.exp(differ), 0.0)
    scores = contract("ovin,ovjn->ovij", readers, writes)
    mixing = scores[:, :, None] * decay_mat
    return (running, final_log, decay_mat, mixing)


def segment_forward(pieces, signal, writes, readers, memory):
    running, final_log, decay_mat, mixing = pieces
    rising = jnp.exp(running)
    falling = jnp.exp(final_log[..., None] - running)
    outputs = contract("ovhij,ovjhp->ovihp", mixing, signal) + contract(
        "ovhi,ovin,ovhnp->ovihp", rising, readers, memory
    )
    memory_next = jnp.exp(final_log)[..., None, None] * memory + contract(
        "ovhj,ovjn,ovjhp->ovhnp", falling, writes, signal
    )
    return (outputs, memory_next)


def segment_backward(pieces, signal, writes, readers, upstream, memory, memory_grad):
    running, final_log, decay_mat, mixing = pieces
    rising = jnp.exp(running)
    falling = jnp.exp(final_log[..., None] - running)
    grad_signal = contract("ovhij,ovihp->ovjhp", mixing, upstream) + contract(
        "ovhj,ovjn,ovhnp->ovjhp", falling, writes, memory_grad
    )
    weighted = contract("ovihp,ovjhp->ovhij", upstream, signal) * decay_mat
    grad_writes = contract("ovhij,ovin->ovjn", weighted, readers) + contract(
        "ovhj,ovjhp,ovhnp->ovjn", falling, signal, memory_grad
    )
    grad_readers = contract("ovhij,ovjn->ovin", weighted, writes) + contract(
        "ovhi,ovihp,ovhnp->ovin", rising, upstream, memory
    )
    grad_prev = jnp.exp(final_log)[..., None, None] * memory_grad + contract(
        "ovhi,ovin,ovihp->ovhnp", rising, readers, upstream
    )
    return (grad_signal, grad_writes, grad_readers, grad_prev)


def run_segments(signal, writes, readers, log_rates, upstream, memory_in, grad_in, length):
    blocks = signal.shape[2] // length

    def cut_rows(array, number, along):
        start_row = (number * length).astype(jnp.int32)
        return lax.dynamic_slice_in_dim(array, start_row, length, along)

    def forward_turn(number, carried):
        memory, outputs, memories = carried
        sig = cut_rows(signal, number, 2)
        wri = cut_rows(writes, number, 2)
        rea = cut_rows(readers, number, 2)
        pieces = segment_parts(cut_rows(log_rates, number, 3), wri, rea)
        out_rows, memory_next = segment_forward(pieces, sig, wri, rea, memory)
        outputs = lax.dynamic_update_slice_in_dim(
            outputs, out_rows, (number * length).astype(jnp.int32), 2
        )
        memories = lax.dynamic_update_index_in_dim(memories, memory, number, 0)
        return (memory_next, outputs, memories)

    start_memories = jnp.zeros((blocks,) + memory_in.shape, memory_in.dtype)
    _, outputs, memories = lax.fori_loop(
        0, blocks, forward_turn, (memory_in, jnp.zeros_like(signal), start_memories)
    )

    def backward_turn(countdown, carried):
        memory_grad, grad_signal, grad_writes, grad_readers = carried
        number = blocks - 1 - countdown
        sig = cut_rows(signal, number, 2)
        wri = cut_rows(writes, number, 2)
        rea = cut_rows(readers, number, 2)
        pieces = segment_parts(cut_rows(log_rates, number, 3), wri, rea)
        memory = lax.dynamic_index_in_dim(memories, number, 0, keepdims=False)
        part_sig, part_wri, part_rea, grad_prev = segment_backward(
            pieces, sig, wri, rea, cut_rows(upstream, number, 2), memory, memory_grad
        )
        start_row = (number * length).astype(jnp.int32)
        grad_signal = lax.dynamic_update_slice_in_dim(grad_signal, part_sig, start_row, 2)
        grad_writes = lax.dynamic_update_slice_in_dim(grad_writes, part_wri, start_row, 2)
        grad_readers = lax.dynamic_update_slice_in_dim(grad_readers, part_rea, start_row, 2)
        return (grad_prev, grad_signal, grad_writes, grad_readers)

    _, grad_signal, grad_writes, grad_readers = lax.fori_loop(
        0,
        blocks,
        backward_turn,
        (grad_in, jnp.zeros_like(signal), jnp.zeros_like(writes), jnp.zeros_like(readers)),
    )
    return (outputs, grad_signal, grad_writes, grad_readers)


def carry_forward(earlier, later):
    return (earlier[0] + later[0], jnp.exp(later[0])[..., None, None] * earlier[1] + later[1])


def carry_backward(earlier, later):
    return (earlier[0] + later[0], later[1] + jnp.exp(later[0])[..., None, None] * earlier[1])


def shards(head_inputs, write_read, decay_steps, scan_orders, cotangent, out_weight):
    volumes, tokens, model_width = cotangent.shape
    ctx_count = lax.axis_size("ctx")
    seq_len = tokens * ctx_count
    local_heads = decay_steps.shape[2]
    inner_width = head_inputs.shape[3]
    gathered = lax.all_gather(cotangent, "ctx", axis=1, tiled=True)

    def reorder(ordering):
        return jax.vmap(lambda table_rows, row_ids: table_rows[row_ids])(gathered, ordering)

    scanned = jnp.stack([cotangent, reorder(scan_orders[0]), reorder(scan_orders[1])])
    upstream = jnp.einsum(
        "ovtd,odi->ovti",
        scanned,
        lax.all_gather(out_weight, "ctx", axis=1, tiled=True),
        preferred_element_type=jnp.float32,
    ).astype(jnp.bfloat16)
    upstream = lax.optimization_barrier(upstream)
    signal = head_inputs.astype(jnp.float32).reshape(3, volumes, tokens, local_heads, P_SIZE)
    grad_up = upstream.astype(jnp.float32).reshape(3, volumes, tokens, local_heads, P_SIZE)
    writes = write_read[..., :N].astype(jnp.float32)
    readers = write_read[..., N:].astype(jnp.float32)
    log_rates = -decay_steps.astype(jnp.float32) / seq_len
    running = jnp.cumsum(log_rates, axis=-1)
    summed_log = running[..., -1]
    end_state = contract(
        "ovht,ovtn,ovthp->ovhnp", jnp.exp(summed_log[..., None] - running), writes, signal
    )
    start_grad = contract("ovht,ovtn,ovthp->ovhnp", jnp.exp(running), readers, grad_up)
    zeros_log = jnp.zeros_like(summed_log)
    zeros_state = jnp.zeros_like(end_state)
    _, state_in = prefix(
        (summed_log, end_state), "ctx", carry_forward, (zeros_log, zeros_state), False
    )
    _, grad_out = prefix(
        (summed_log, start_grad), "ctx", carry_backward, (zeros_log, zeros_state), True
    )
    length = math.gcd(tokens, 128)
    outputs, grad_signal, grad_writes, grad_readers = run_segments(
        signal, writes, readers, log_rates, grad_up, state_in, grad_out, length
    )
    grad_wr = lax.psum(jnp.concatenate([grad_writes, grad_readers], axis=-1), "mp").astype(
        jnp.bfloat16
    )
    grad_inputs = grad_signal.reshape(3, volumes, tokens, inner_width).astype(jnp.bfloat16)
    outputs_bf = outputs.reshape(3, volumes, tokens, inner_width).astype(jnp.bfloat16)
    weight_term = jnp.einsum(
        "ovtd,ovti->odi", scanned, outputs_bf, preferred_element_type=jnp.float32
    )
    rows_sum = lax.psum_scatter(weight_term, "ctx", scatter_dimension=1, tiled=True)
    weight_grad = lax.psum(rows_sum, "dp").astype(jnp.bfloat16)
    return (grad_inputs, grad_wr, weight_grad)


def solution(mesh):
    in_specs = (
        P(None, ("groups", "dp"), "ctx", "mp"),
        P(None, ("groups", "dp"), "ctx", None),
        P(None, ("groups", "dp"), "mp", "ctx"),
        P(None, ("groups", "dp"), "ctx"),
        P(("groups", "dp"), "ctx", None),
        P(None, "ctx", "mp"),
    )
    out_specs = (
        P(None, ("groups", "dp"), "ctx", "mp"),
        P(None, ("groups", "dp"), "ctx", None),
        P("groups", "ctx", "mp"),
    )
    return jax.shard_map(shards, mesh=mesh, in_specs=in_specs, out_specs=out_specs, check_vma=False)
```

profile of v0, /device:TPU:0, one launch (start us, length us, event | category | flops | bytes accessed | tf_op | source)
XLA Modules:
  0.0 406.5 jit_solution(13065868097995965039)
XLA Ops:
  8.7 5.4 %reduce-window.6 = f32[3,1,6,2,128]{4,3,2,1,0:T(2,128)S(1)} reduce-window(f32[3,1,6,2,128]{4,3,2,1,0:T(2,128)S(1)} %bitcast.295, f32[]{:T(128)} %constant.173.clone.1), window={size=1x1x1x1x128 pad=0_0x0_0x0_0x0_0x127_0}, to_apply=%region_0.0 | reduce-window | flops 585216 | bytes 36868 | tf_op jit(solution)/shard_map/reduce-window
  18.4 2.2 fusion.72
  23.2 14.1 %all-gather.1 = f32[12,1,6,1]{2,3,1,0:T(1,128)} all-gather(f32[3,1,6,1]{2,3,1,0:T(1,128)S(1)} %copy.107), channel_id=3, replica_groups=mesh['groups'=2,'ctx'=4,'dp'=2,'mp'=2] {'ctx'}, dimensions={0}, use_global_device_ids=true | all-gather | bytes 360 | tf_op jit(solution)/shard_map/all_gather | solution.py:14
  37.3 12.2 %all-gather.8.cloned.1.call-done = bf16[1,1024,768]{2,1,0:T(8,128)(2,1)} async-done(((bf16[1,256,768]{2,1,0:T(8,128)(2,1)}), bf16[1,1024,768]{2,1,0:T(8,128)(2,1)}) %all-gather.8.cloned.1.call-update) | async-done | bytes 1572880 | tf_op jit(solution)/shard_map/all_gather | solution.py:143
  49.6 3.6 gather_fusion
  53.2 2.9 gather_fusion.1
  56.1 45.0 %all-gather.14.cloned.1.call-done = f32[12,6,64,128]{3,2,1,0:T(8,128)} async-done(((f32[3,6,64,128]{3,2,1,0:T(8,128)}), f32[12,6,64,128]{3,2,1,0:T(8,128)}) %all-gather.14.cloned.1.call-update) | async-done | bytes 2359312 | tf_op jit(solution)/shard_map/all_gather | solution.py:14
  101.1 5.7 %while.69 = (s32[]{:T(128)}, f32[3,1,6,64,128]{4,3,2,1,0:T(8,128)S(1)}, s32[]{:T(128)}, f32[4,3,1,6]{3,2,1,0:T(1,128)}, f32[4,3,1,6,64,128]{5,4,3,1,2,0:T(8,128)}, /*index=5*/s32[]{:T(128)}, s32[]{:T(128)}) while((s32[]{:T(128)}, f32[3,1,6,64,128]{4,3,2,1,0:T(8,128)S(1)}, s32[]{:T(128)}, f32[4,3,1,6]{3,2,1,0:T(1,128)}, ...), condition=%wide.region_5.6_spmd.clone, body=%wide.region_4.5_spmd.clone.sunk | while | flops 589828 | bytes 1769937 | solution.py:26
  106.8 64.7 %all-gather.10.cloned.1.call-done = bf16[3,768,768]{2,1,0:T(8,128)(2,1)} async-done(((bf16[3,192,768]{2,1,0:T(8,128)(2,1)}), bf16[3,768,768]{2,1,0:T(8,128)(2,1)}) %all-gather.10.cloned.1.call-update) | async-done | bytes 3538960 | tf_op jit(solution)/shard_map/all_gather | solution.py:152
  171.5 3.3 fusion.71
  176.3 3.5 fusion.74
  180.2 27.0 %while.66 = (s32[]{:T(128)}, f32[3,1,6,64,128]{4,3,2,0,1:T(8,128)S(1)}, bf16[3,1,256,6,128]{2,4,3,0,1:T(8,128)(2,1)S(1)}, f32[2,3,1,6,64,128]{5,4,3,1,2,0:T(8,12...) while((s32[]{:T(128)}, ...), condition=%wide.region_8.9_spmd, body=%wide.region_6.8_spmd.sunk | while | flops 946094080 | bytes 10168943 | solution.py:99
  184.6 2.0 convolution_bitcast_fusion.8
  187.1 3.9 fusion.159
  191.2 2.5 fusion.157
  200.6 3.9 fusion.159
  204.6 2.5 fusion.157
  207.2 5.7 %fusion.82 = f32[3,768,768]{2,1,0:T(8,128)} fusion(bf16[3,256,768]{1,2,0:T(8,128)(2,1)S(1)} %bitcast.282, bf16[1,1,256,768]{3,2,0,1:T(8,128)(2,1)} %bitcast.290, bf16[1,1,256,768]{3,2,0,1:T(8,128)(2,1)S(1)} %bitcast.288, bf16[1,1,256,768]{3,2,0,1:T(8,128)(2,1)} %bitcast.292), kind=kOutput, calls=%fused_computation.120 | convolution fusion | flops 907149312 | bytes 9437184 | tf_op jit(solution)/shard_map/ovtd,ovti->odi/dot_general | solution.py:184
  216.0 13.1 %all-gather.12.cloned.1.call-done = f32[12,6,64,128]{3,2,1,0:T(8,128)} async-done(((f32[3,6,64,128]{3,2,1,0:T(8,128)}), f32[12,6,64,128]{3,2,1,0:T(8,128)}) %all-gather.12.cloned.1.call-update) | async-done | bytes 2359312 | tf_op jit(solution)/shard_map/all_gather | solution.py:14
  233.1 41.1 %while.67 = (s32[]{:T(128)}, f32[3,1,6,64,128]{4,3,2,0,1:T(8,128)S(1)}, bf16[3,1,256,6,128]{2,4,3,0,1:T(8,128)(2,1)S(1)}, f32[3,1,256,64]{2,3,0,1:T(8,128)}, f32...) while((s32[]{:T(128)}, ...), condition=%wide.region_12.13_spmd, body=%wide.region_9.12_spmd.sunk | while | flops 1929625600 | bytes 41488220 | solution.py:120
  241.0 2.3 fusion.182
  243.3 3.7 fusion.180
  247.5 2.6 fusion.179
  250.2 2.4 fusion.176
  255.7 2.0 convolution_bitcast_fusion.9
  261.5 2.3 fusion.182
  263.8 3.7 fusion.180
  268.0 2.7 fusion.179
  270.7 2.4 fusion.176
  278.0 5.0 %all-reduce.2 = bf16[3,1,256,128]{3,2,1,0:T(8,128)(2,1)} all-reduce(f32[3,1,256,128]{3,2,1,0:T(8,128)S(1)} %pad_maximum_fusion), channel_id=1, replica_groups=mesh['groups'=2,'ctx'=4,'dp'=2,'mp'=2] {'mp'}, use_global_device_ids=true, to_apply=%region_13.14 | all-reduce | flops 98304 | bytes 589824 | tf_op jit(solution)/shard_map/psum | solution.py:179
  283.0 70.6 %reduce-scatter.2.cloned.1.call-done = f32[3,192,768]{2,1,0:T(8,128)} async-done(((f32[3,768,768]{2,1,0:T(8,128)}), f32[3,192,768]{2,1,0:T(8,128)}) %reduce-scatter.2.cloned.1.call-update) | async-done | bytes 1769488 | tf_op jit(solution)/shard_map/reduce_scatter | solution.py:187
  353.6 46.3 %all-reduce.3 = bf16[3,192,768]{2,1,0:T(8,128)(2,1)} all-reduce(f32[3,192,768]{2,1,0:T(8,128)} %reduce-scatter.2.cloned.1.call-done), channel_id=1, replica_groups=mesh['groups'=2,'ctx'=4,'dp'=2,'mp'=2] {'dp'}, use_global_device_ids=true, to_apply=%region_15.16 | all-reduce | flops 442368 | bytes 2654208 | tf_op jit(solution)/shard_map/psum | solution.py:188
  (153 shorter events, 55.7 us)
Async XLA Ops:
  7.2 8.9 %copy-start.10 = (bf16[3,1,256,768]{3,2,1,0:T(8,128)(2,1)S(1)}, bf16[3,1,256,768]{3,2,1,0:T(8,128)(2,1)}, u32[]{:S(2)}) copy-start(bf16[3,1,256,768]{3,2,1,0:T(8,128)(2,1)} %param.14) | copy-start | bytes 3538948
  7.2 42.4 %all-gather.8.cloned.1.call-start = ((), (), s32[]{:S(2)}) async-start(), calls=%async_computation.1 | async-start | bytes 1966080 | tf_op jit(solution)/shard_map/all_gather | solution.py:143
  7.9 93.2 %all-gather.14.cloned.1.call-start = ((), (), s32[]{:S(2)}) async-start(), calls=%async_computation.5 | async-start | bytes 2949120 | tf_op jit(solution)/shard_map/all_gather | solution.py:14
  8.7 8.0 %copy-start.8 = (f32[3,1,6,256]{3,2,1,0:T(8,128)}, f32[3,1,6,256]{3,2,1,0:T(8,128)S(1)}, u32[]{:S(2)}) copy-start(f32[3,1,6,256]{3,2,1,0:T(8,128)S(1)} %fusion.84) | copy-start | bytes 55300
  20.6 150.9 %all-gather.10.cloned.1.call-start = ((), (), s32[]{:S(2)}) async-start(), calls=%async_computation.2 | async-start | bytes 4423680 | tf_op jit(solution)/shard_map/all_gather | solution.py:152
  21.3 207.8 %all-gather.12.cloned.1.call-start = ((), (), s32[]{:S(2)}) async-start(), calls=%async_computation.4 | async-start | bytes 2949120 | tf_op jit(solution)/shard_map/all_gather | solution.py:14
  21.5 15.8 %copy-start.14 = (s32[2,1,256]{2,1,0:T(1,128)S(1)}, s32[2,1,256]{2,1,0:T(1,128)}, u32[]{:S(2)}) copy-start(s32[2,1,256]{2,1,0:T(1,128)} %param.17) | copy-start | bytes 6148
  49.6 3.7 copy-start.1
  101.1 70.4 %copy-start.7 = (bf16[256,768]{1,0:T(8,128)(2,1)S(1)}, bf16[256,768]{1,0:T(8,128)(2,1)}, u32[]{:S(2)}) copy-start(bf16[256,768]{1,0:T(8,128)(2,1)} %gather_fusion) | copy-start | bytes 1179652
  174.8 1.5 copy-start.3
  179.8 173.8 %reduce-scatter.2.cloned.1.call-start = ((), (), s32[]{:S(2)}) async-start(), calls=%async_computation.3 | async-start | bytes 8847360 | tf_op jit(solution)/shard_map/reduce_scatter | solution.py:187
  207.2 5.8 %copy-start.2 = (f32[2,3,1,6,64,128]{5,4,3,1,2,0:T(8,128)}, f32[2,3,1,6,64,128]{5,4,3,1,2,0:T(8,128)S(1)}, u32[]{:S(2)}) copy-start(f32[2,3,1,6,64,128]{5,4,3,1,2,0:T(8,128)S(1)} %get-tuple-element.1132) | copy-start | bytes 3538948
  212.9 0.7 copy-start.13
  212.9 1.3 copy-start.4
  231.5 1.5 copy-start.9
  234.1 3.6 copy-start
  239.6 1.0 copy-start.5
  243.3 3.7 copy-start.11
  247.5 2.6 copy-start.12
  250.2 3.4 copy-start.6
  254.6 3.6 copy-start
  260.1 1.0 copy-start.5
  263.8 3.7 copy-start.11
  268.0 2.7 copy-start.12
  270.7 3.4 copy-start.6
Sparse Core Ops, SparseCore 0:
  9.6 39.9 all-gather.7
  51.7 49.3 all-gather.13
  102.7 68.7 all-gather.9
  180.0 49.1 all-gather.11
  231.3 122.3 reduce-scatter.1
where the time goes:
time: 408 us; the launch traced here: 406 us
  waiting for transfers between devices  207 us (51%)
  matrix products  66.1 us (16%)
  blocking collectives  65.4 us (16%)
  local copies, waits for them, and re-layouts  35.1 us (9%)
  other arithmetic  18 us (4%)
  between operations  14 us (3%)
    reduce_scatter x1, waiting for transfers between devices, shards(): lax.psum_scatter(weight_term, 'ctx', scatter_dimension=1, tiled=True)  70.6 us
    all_gather x1, waiting for transfers between devices, shards(): lax.all_gather(out_weight, 'ctx', axis=1, tiled=True)  64.7 us
    all_gather x2, waiting for transfers between devices, prefix(): pieces = jax.tree.map(lambda part: lax.all_gather(part, axis), value)  58.1 us
    dot_general x28, matrix products, contract(): return jnp.einsum(form, *operands, precision=EXACT)  57 us
    psum x1, blocking collectives, shards(): weight_grad = lax.psum(rows_sum, 'dp').astype(jnp.bfloat16)  46.3 us
    all_gather x1, blocking collectives, prefix(): pieces = jax.tree.map(lambda part: lax.all_gather(part, axis), value)  14.1 us
    all_gather x1, waiting for transfers between devices, shards(): gathered = lax.all_gather(cotangent, 'ctx', axis=1, tiled=True)  12.2 us
  transfers between devices with their start and end apart: 5, of which 5 were waited for; matrix products, arithmetic and copies ran while one was open for 26% of the time, Pallas kernels for 0%

commit v1 on v0

--- a/solution.py
+++ b/solution.py
@@ -140,7 +140,14 @@
     seq_len = tokens * ctx_count
     local_heads = decay_steps.shape[2]
     inner_width = head_inputs.shape[3]
-    gathered = lax.all_gather(cotangent, "ctx", axis=1, tiled=True)
+    n_dev = lax.axis_size("ctx")
+    right = [(i, (i + 1) % n_dev) for i in range(n_dev)]
+    parts = [cotangent]
+    for far in range(1, n_dev):
+        parts = [lax.ppermute(parts[0], "ctx", right), *parts]
+    out = jnp.concatenate(parts, axis=1)
+    places = (lax.axis_index("ctx") + 1) * parts[-1].shape[1]
+    gathered = jnp.roll(out, places, axis=1)
 
     def reorder(ordering):
         return jax.vmap(lambda table_rows, row_ids: table_rows[row_ids])(gathered, ordering)

time: 408 us -> 395 us (0.968)
  waiting for transfers between devices: 207 us -> 163 us
  blocking collectives: 65.4 us -> 86.8 us
  starting transfers between devices: 0.38 us -> 5.53 us
    all_gather x2, waiting for transfers between devices: 58.1 us -> 13.1 us  [prefix(): pieces = jax.tree.map(lambda part: lax.all_gather(part, axis), value)]
    ppermute x0 -> x3, waiting for transfers between devices: none -> 26.6 us  [shards(): parts = [lax.ppermute(parts[0], 'ctx', right), *parts]]
    all_gather x1, blocking collectives: 14.1 us -> 35.5 us  [prefix(): pieces = jax.tree.map(lambda part: lax.all_gather(part, axis), value)]
    all_gather x1, waiting for transfers between devices: 64.7 us -> 52.4 us  [shards(): lax.all_gather(out_weight, 'ctx', axis=1, tiled=True)]
    all_gather x1 -> x0, waiting for transfers between devices: 12.2 us -> none  [shards(): gathered = lax.all_gather(cotangent, 'ctx', axis=1, tiled=True)]
    ppermute x0 -> x3, starting transfers between devices: none -> 5.19 us  [shards(): parts = [lax.ppermute(parts[0], 'ctx', right), *parts]]
    unnamed x24 -> x31, local copies, waits for them, and re-layouts: 3.73 us -> 8.07 us
  transfers between devices with their start and end apart: 5 -> 7, of which waited for: 5 -> 5; matrix products, arithmetic and copies ran while one was open for 26% -> 25% of each run, Pallas kernels for 0% -> 0%
where the time goes in v1:
time: 395 us; the launch traced here: 393 us
  waiting for transfers between devices  163 us (41%)
  blocking collectives  86.8 us (22%)
  matrix products  66.1 us (17%)
  local copies, waits for them, and re-layouts  38.8 us (10%)
  other arithmetic  18.1 us (5%)
  between operations  14 us (4%)
  starting transfers between devices  5.53 us (1%)
    reduce_scatter x1, waiting for transfers between devices, shards(): lax.psum_scatter(weight_term, 'ctx', scatter_dimension=1, tiled=True)  70.6 us
    dot_general x28, matrix products, contract(): return jnp.einsum(form, *operands, precision=EXACT)  57 us
    all_gather x1, waiting for transfers between devices, shards(): lax.all_gather(out_weight, 'ctx', axis=1, tiled=True)  52.4 us
    psum x1, blocking collectives, shards(): weight_grad = lax.psum(rows_sum, 'dp').astype(jnp.bfloat16)  46.3 us
    all_gather x1, blocking collectives, prefix(): pieces = jax.tree.map(lambda part: lax.all_gather(part, axis), value)  35.5 us
    ppermute x3, waiting for transfers between devices, shards(): parts = [lax.ppermute(parts[0], 'ctx', right), *parts]  26.6 us
    all_gather x2, waiting for transfers between devices, prefix(): pieces = jax.tree.map(lambda part: lax.all_gather(part, axis), value)  13.1 us
    unnamed x31, local copies, waits for them, and re-layouts  8.07 us
  transfers between devices with their start and end apart: 7, of which 5 were waited for; matrix products, arithmetic and copies ran while one was open for 25% of the time, Pallas kernels for 0%

profile of v1, /device:TPU:0, one launch (start us, length us, event | category | flops | bytes accessed | tf_op | source)
XLA Modules:
  0.0 393.5 jit_solution(15858566617171104322)
XLA Ops:
  8.1 5.4 %reduce-window.6 = f32[3,1,6,2,128]{4,3,2,1,0:T(2,128)S(1)} reduce-window(f32[3,1,6,2,128]{4,3,2,1,0:T(2,128)S(1)} %bitcast.295, f32[]{:T(128)} %constant.193.clone.1), window={size=1x1x1x1x128 pad=0_0x0_0x0_0x0_0x127_0}, to_apply=%region_0.1 | reduce-window | flops 585216 | bytes 36868 | tf_op jit(solution)/shard_map/reduce-window
  17.7 2.2 fusion.72
  20.9 3.0 collective-permute-start
  23.9 11.4 %collective-permute-done = bf16[1,256,768]{2,1,0:T(8,128)(2,1)} collective-permute-done((bf16[1,256,768]{2,1,0:T(8,128)(2,1)S(1)}, bf16[1,256,768]{2,1,0:T(8,128)(2,1)}, u32[]{:S(2)}, u32[]{:S(2)}) %collective-permute-start) | collective-permute-done | bytes 393248 | tf_op jit(solution)/shard_map/ppermute | solution.py:147
  35.3 2.1 collective-permute-start.1
  39.2 35.5 %all-gather.1 = f32[12,1,6,1]{2,3,1,0:T(1,128)} all-gather(f32[3,1,6,1]{2,3,1,0:T(1,128)S(1)} %copy.107), channel_id=3, replica_groups=mesh['groups'=2,'ctx'=4,'dp'=2,'mp'=2] {'ctx'}, dimensions={0}, use_global_device_ids=true | all-gather | bytes 360 | tf_op jit(solution)/shard_map/all_gather | solution.py:14
  74.9 15.2 %collective-permute-done.2 = bf16[1,256,768]{2,1,0:T(8,128)(2,1)S(1)} collective-permute-done((bf16[1,256,768]{2,1,0:T(8,128)(2,1)}, bf16[1,256,768]{2,1,0:T(8,128)(2,1)S(1)}, u32[]{:S(2)}, u32[]{:S(2)}) %collective-permute-start.2) | collective-permute-done | bytes 393248 | tf_op jit(solution)/shard_map/ppermute | solution.py:147
  94.5 2.9 gather_fusion
  97.4 2.9 gather_fusion.1
  100.3 5.8 %while.69 = (s32[]{:T(128)}, f32[3,1,6,64,128]{4,3,2,1,0:T(8,128)S(1)}, s32[]{:T(128)}, f32[4,3,1,6]{3,2,1,0:T(1,128)}, f32[4,3,1,6,64,128]{5,4,3,1,2,0:T(8,128)}, /*index=5*/s32[]{:T(128)}, s32[]{:T(128)}) while((s32[]{:T(128)}, f32[3,1,6,64,128]{4,3,2,1,0:T(8,128)S(1)}, s32[]{:T(128)}, f32[4,3,1,6]{3,2,1,0:T(1,128)}, ...), condition=%wide.region_5.6_spmd.clone, body=%wide.region_4.5_spmd.clone.sunk | while | flops 589828 | bytes 1769937 | solution.py:26
  106.0 52.4 %all-gather.7.cloned.1.call-done = bf16[3,768,768]{2,1,0:T(8,128)(2,1)} async-done(((bf16[3,192,768]{2,1,0:T(8,128)(2,1)}), bf16[3,768,768]{2,1,0:T(8,128)(2,1)}) %all-gather.7.cloned.1.call-update) | async-done | bytes 3538960 | tf_op jit(solution)/shard_map/all_gather | solution.py:159
  158.4 3.4 fusion.71
  163.3 3.6 fusion.74
  167.2 27.0 %while.66 = (s32[]{:T(128)}, f32[3,1,6,64,128]{4,3,2,0,1:T(8,128)S(1)}, bf16[3,1,256,6,128]{2,4,3,0,1:T(8,128)(2,1)S(1)}, f32[2,3,1,6,64,128]{5,4,3,1,2,0:T(8,12...) while((s32[]{:T(128)}, ...), condition=%wide.region_8.9_spmd, body=%wide.region_6.8_spmd.sunk | while | flops 946094080 | bytes 10168943 | solution.py:99
  174.1 3.9 fusion.159
  178.2 2.5 fusion.157
  187.6 3.9 fusion.159
  191.6 2.5 fusion.157
  194.2 5.7 %fusion.82 = f32[3,768,768]{2,1,0:T(8,128)} fusion(bf16[3,256,768]{1,2,0:T(8,128)(2,1)S(1)} %bitcast.282, bf16[1,1,256,768]{3,2,0,1:T(8,128)(2,1)} %bitcast.292, bf16[1,1,256,768]{3,2,0,1:T(8,128)(2,1)} %bitcast.290, bf16[1,1,256,768]{3,2,0,1:T(8,128)(2,1)S(1)} %bitcast.287), kind=kOutput, calls=%fused_computation.120 | convolution fusion | flops 907149312 | bytes 9437184 | tf_op jit(solution)/shard_map/ovtd,ovti->odi/dot_general | solution.py:191
  203.0 13.1 %all-gather.9.cloned.1.call-done = f32[12,6,64,128]{3,2,1,0:T(8,128)} async-done(((f32[3,6,64,128]{3,2,1,0:T(8,128)}), f32[12,6,64,128]{3,2,1,0:T(8,128)}) %all-gather.9.cloned.1.call-update) | async-done | bytes 2359312 | tf_op jit(solution)/shard_map/all_gather | solution.py:14
  220.0 41.1 %while.67 = (s32[]{:T(128)}, f32[3,1,6,64,128]{4,3,2,0,1:T(8,128)S(1)}, bf16[3,1,256,6,128]{2,4,3,0,1:T(8,128)(2,1)S(1)}, f32[3,1,256,64]{2,3,0,1:T(8,128)}, f32...) while((s32[]{:T(128)}, ...), condition=%wide.region_12.13_spmd, body=%wide.region_9.12_spmd.sunk | while | flops 1929625600 | bytes 41488220 | solution.py:120
  228.0 2.3 fusion.182
  230.3 3.7 fusion.180
  234.5 2.6 fusion.179
  237.2 2.4 fusion.176
  248.5 2.3 fusion.182
  250.8 3.7 fusion.180
  255.0 2.7 fusion.179
  257.7 2.4 fusion.176
  265.0 5.0 %all-reduce.3 = bf16[3,1,256,128]{3,2,1,0:T(8,128)(2,1)} all-reduce(f32[3,1,256,128]{3,2,1,0:T(8,128)S(1)} %pad_maximum_fusion), channel_id=1, replica_groups=mesh['groups'=2,'ctx'=4,'dp'=2,'mp'=2] {'mp'}, use_global_device_ids=true, to_apply=%region_13.14 | all-reduce | flops 98304 | bytes 589824 | tf_op jit(solution)/shard_map/psum | solution.py:186
  270.0 70.6 %reduce-scatter.2.cloned.1.call-done = f32[3,192,768]{2,1,0:T(8,128)} async-done(((f32[3,768,768]{2,1,0:T(8,128)}), f32[3,192,768]{2,1,0:T(8,128)}) %reduce-scatter.2.cloned.1.call-update) | async-done | bytes 1769488 | tf_op jit(solution)/shard_map/reduce_scatter | solution.py:194
  340.6 46.3 %all-reduce.2 = bf16[3,192,768]{2,1,0:T(8,128)(2,1)} all-reduce(f32[3,192,768]{2,1,0:T(8,128)} %reduce-scatter.2.cloned.1.call-done), channel_id=1, replica_groups=mesh['groups'=2,'ctx'=4,'dp'=2,'mp'=2] {'dp'}, use_global_device_ids=true, to_apply=%region_15.16 | all-reduce | flops 442368 | bytes 2654208 | tf_op jit(solution)/shard_map/psum | solution.py:195
  (165 shorter events, 63.7 us)
Async XLA Ops:
  7.2 8.2 %copy-start.10 = (bf16[3,1,256,768]{3,2,1,0:T(8,128)(2,1)S(1)}, bf16[3,1,256,768]{3,2,1,0:T(8,128)(2,1)}, u32[]{:S(2)}) copy-start(bf16[3,1,256,768]{3,2,1,0:T(8,128)(2,1)} %param.14) | copy-start | bytes 3538948
  7.2 93.1 %all-gather.11.cloned.1.call-start = ((), (), s32[]{:S(2)}) async-start(), calls=%async_computation.4 | async-start | bytes 2949120 | tf_op jit(solution)/shard_map/all_gather | solution.py:14
  8.0 8.0 %copy-start.8 = (f32[3,1,6,256]{3,2,1,0:T(8,128)}, f32[3,1,6,256]{3,2,1,0:T(8,128)S(1)}, u32[]{:S(2)}) copy-start(f32[3,1,6,256]{3,2,1,0:T(8,128)S(1)} %fusion.84) | copy-start | bytes 55300
  19.9 1.0 copy-start.6
  19.9 138.5 %all-gather.7.cloned.1.call-start = ((), (), s32[]{:S(2)}) async-start(), calls=%async_computation.1 | async-start | bytes 4423680 | tf_op jit(solution)/shard_map/all_gather | solution.py:159
  20.6 195.5 %all-gather.9.cloned.1.call-start = ((), (), s32[]{:S(2)}) async-start(), calls=%async_computation.3 | async-start | bytes 2949120 | tf_op jit(solution)/shard_map/all_gather | solution.py:14
  20.9 14.4 %collective-permute-start = (bf16[1,256,768]{2,1,0:T(8,128)(2,1)S(1)}, bf16[1,256,768]{2,1,0:T(8,128)(2,1)}, u32[]{:S(2)}, u32[]{:S(2)}) collective-permute-start(bf16[1,256,768]{2,1,0:T(8,128)(2,1)S(1)} %copy-done.6), channel_id=1, source_target_pairs={{0,4},{4,8},{8,12},{12,0},{1,5},{5,9},{9,13},{13,1},{2,6},{6,10},{... | collective-permute-start | bytes 1179656 | tf_op jit(solution)/shard_map/ppermute | solution.py:147
  35.3 39.5 %collective-permute-start.1 = (bf16[1,256,768]{2,1,0:T(8,128)(2,1)}, bf16[1,256,768]{2,1,0:T(8,128)(2,1)}, u32[]{:S(2)}, u32[]{:S(2)}) collective-permute-start(bf16[1,256,768]{2,1,0:T(8,128)(2,1)} %collective-permute-done), channel_id=1, source_target_pairs={{0,4},{4,8},{8,12},{12,0},{1,5},{5,9},{9,13},{13,1},{2,6},{6,10},{... | collective-permute-start | bytes 1179656 | tf_op jit(solution)/shard_map/ppermute | solution.py:147
  37.5 37.3 %copy-start.14 = (s32[2,1,256]{2,1,0:T(1,128)S(1)}, s32[2,1,256]{2,1,0:T(1,128)}, u32[]{:S(2)}) copy-start(s32[2,1,256]{2,1,0:T(1,128)} %param.17) | copy-start | bytes 6148
  74.8 15.3 %collective-permute-start.2 = (bf16[1,256,768]{2,1,0:T(8,128)(2,1)}, bf16[1,256,768]{2,1,0:T(8,128)(2,1)S(1)}, u32[]{:S(2)}, u32[]{:S(2)}) collective-permute-start(bf16[1,256,768]{2,1,0:T(8,128)(2,1)} %collective-permute-done.1), channel_id=1, source_target_pairs={{0,4},{4,8},{8,12},{12,0},{1,5},{5,9},{9,13},{13,1},{2,6},{6,10},{... | collective-permute-start | bytes 1179656 | tf_op jit(solution)/shard_map/ppermute | solution.py:147
  100.3 58.1 %copy-start.7 = (bf16[1,256,768]{2,1,0:T(8,128)(2,1)S(1)}, bf16[1,256,768]{2,1,0:T(8,128)(2,1)}, u32[]{:S(2)}) copy-start(bf16[1,256,768]{2,1,0:T(8,128)(2,1)} %param.18) | copy-start | bytes 1179652
  161.8 1.5 copy-start.2
  166.8 173.8 %reduce-scatter.2.cloned.1.call-start = ((), (), s32[]{:S(2)}) async-start(), calls=%async_computation.2 | async-start | bytes 8847360 | tf_op jit(solution)/shard_map/reduce_scatter | solution.py:194
  194.2 5.7 %copy-start.1 = (f32[2,3,1,6,64,128]{5,4,3,1,2,0:T(8,128)}, f32[2,3,1,6,64,128]{5,4,3,1,2,0:T(8,128)S(1)}, u32[]{:S(2)}) copy-start(f32[2,3,1,6,64,128]{5,4,3,1,2,0:T(8,128)S(1)} %get-tuple-element.1132) | copy-start | bytes 3538948
  199.9 0.7 copy-start.13
  199.9 1.3 copy-start.3
  218.5 1.5 copy-start.9
  221.1 3.6 copy-start
  226.6 1.0 copy-start.4
  230.3 3.7 copy-start.11
  234.5 2.6 copy-start.12
  237.2 3.4 copy-start.5
  241.6 3.6 copy-start
  247.1 1.0 copy-start.4
  250.8 3.7 copy-start.11
  255.0 2.7 copy-start.12
  257.7 3.4 copy-start.5
Sparse Core Ops, SparseCore 0:
  20.0 68.4 all-gather.10
  90.1 68.3 all-gather.6
  167.0 49.1 all-gather.8
  218.3 122.3 reduce-scatter.1
